TPU v7x, 512 devices: a whole 4x8x8 slice. The times are simulated.
512 devices in a mesh: rep: 64 (over z_lo, y, x), fsdp: 8 (over z_hi, core).
Axes of the slice: x: 4, y: 8, z: 8 (z_hi: 4, z_lo: 2; z = z_hi * 2 + z_lo), core: 2. Of those that a mesh axis runs over, the one named last changes fastest.
Arguments:
- inner_weights: float32 [64, 256, 4608], P('rep', 'fsdp'), may hold values from -16 to 16
- grads: bfloat16 [64, 256, 4608], P('rep', 'fsdp'), may hold values from -6000 to 6000
- first_moment: float32 [64, 256, 4608], P('rep', 'fsdp'), may hold values from -1.5 to 1.5
- second_moment: float32 [64, 256, 4608], P('rep', 'fsdp'), may hold values from 0.001 to 0.05
- anchor: float32 [256, 4608], P('fsdp', 'rep'), may hold values from -6 to 6
- outer_momentum: float32 [256, 4608], P('fsdp', 'rep'), may hold values from -4 to 4
Outputs:
- new_params: float32 [256, 4608], P('fsdp')
- new_momentum: float32 [256, 4608], P('fsdp', 'rep')
- new_first: float32 [64, 256, 4608], P('rep', 'fsdp')
- new_second: float32 [64, 256, 4608], P('rep', 'fsdp')
All inputs are finite; a program needn't handle non-finite values.
Results may differ from a plain program's by a relative error of at most 0.0018.
Values sent between devices are 32-bit elements; how exact they have to be, the bound alone decides.
No kernel may reach another device: no remote copies, remote signals or barrier semaphores. Data moves between devices by JAX's collectives and lax.ppermute only.
A program may use at most 64 MiB of HBM per device.

v0:
```python
import math

import jax
import jax.numpy as jnp
from jax import lax
from jax.sharding import PartitionSpec as P

beta_one = 0.9
beta_two = 0.95
inner_rate = 0.01
weight_decay = 0.1
adam_eps = 1e-08
clip_rms = 0.5
outer_rate = 0.7
outer_beta = 0.9


def body(inner_weights, grads, first_moment, second_moment, anchor, outer_momentum):
    gradient = grads.astype(jnp.float32)
    partial_sum = jnp.sum(gradient * gradient)
    norm_square = lax.psum(partial_sum, "fsdp")
    entries = grads.shape[1] * grads.shape[2] * lax.axis_size("fsdp")
    clip_factor = jnp.minimum(1.0, clip_rms * math.sqrt(entries) / jnp.sqrt(norm_square + 1e-06))
    clipped = gradient * clip_factor
    new_first = beta_one * first_moment + (1.0 - beta_one) * clipped
    new_second = beta_two * second_moment + (1.0 - beta_two) * clipped * clipped
    stepped = inner_weights - inner_rate * (
        new_first / (jnp.sqrt(new_second) + adam_eps) + weight_decay * inner_weights
    )
    replicas = lax.axis_size("rep")
    summed = lax.psum(stepped[0], "rep")
    full_anchor, full_momentum = (
        lax.all_gather(anchor, "rep", axis=1, tiled=True),
        lax.all_gather(outer_momentum, "rep", axis=1, tiled=True),
    )
    change = full_anchor - summed / replicas
    momentum_full = outer_beta * full_momentum + change
    new_params = full_anchor - outer_rate * (change + outer_beta * momentum_full)
    columns = anchor.shape[1]
    new_momentum = lax.dynamic_slice_in_dim(
        momentum_full, lax.axis_index("rep") * columns, columns, 1
    )
    return (new_params, new_momentum, new_first, new_second)


def solution(mesh):
    placed = (
        P("rep", "fsdp", None),
        P("rep", "fsdp", None),
        P("rep", "fsdp", None),
        P("rep", "fsdp", None),
        P("fsdp", "rep"),
        P("fsdp", "rep"),
    )
    return jax.shard_map(
        body,
        mesh=mesh,
        in_specs=placed,
        out_specs=(
            P("fsdp", None),
            P("fsdp", "rep"),
            P("rep", "fsdp", None),
            P("rep", "fsdp", None),
        ),
        check_vma=False,
    )
```

profile of v0, /device:TPU:64, one launch (start us, length us, event | category | flops | bytes accessed | tf_op | source)
XLA Modules:
  0.0 607.1 jit_solution(16400582454270150556)
XLA Ops:
  7.2 0.0 copy-start
  7.2 0.0 all-reduce.2.cloned.1.call-start
  7.2 1.8 fusion.2
  9.0 22.4 %psum.14 = f32[]{:T(128)} all-reduce(f32[]{:T(128)} %fusion.2), channel_id=1, replica_groups=mesh['rep'=64,'fsdp'=8] {'fsdp'}, use_global_device_ids=true, to_apply=%region_1.0 | all-reduce | flops 1 | bytes 8 | tf_op jit(solution)/shard_map/psum | solution.py:21
  32.1 0.0 copy-done
  32.1 2.9 subtract_bitcast_fusion
  35.0 0.0 copy-start.1
  35.0 0.0 all-reduce.2.cloned.1.call-update
  35.0 0.7 copy-done.1
  35.7 161.5 %all-gather = f32[64,72,32]{1,2,0:T(8,128)S(1)} all-gather(f32[1,72,32]{1,2,0:T(8,128)S(1)} %bitcast.25), channel_id=1, replica_groups=mesh['rep'=64,'fsdp'=8] {'rep'}, dimensions={0}, use_global_device_ids=true | all-gather | bytes 599040 | tf_op jit(solution)/shard_map/all_gather | solution.py:33
  197.2 0.6 copy.12
  197.8 0.0 copy-start.2
  197.8 0.5 reshape.9
  198.4 0.2 copy-done.2
  198.5 155.7 %all-gather.1 = f32[64,72,32]{1,2,0:T(8,128)S(1)} all-gather(f32[1,72,32]{1,2,0:T(8,128)S(1)} %bitcast.26), channel_id=1, replica_groups=mesh['rep'=64,'fsdp'=8] {'rep'}, dimensions={0}, use_global_device_ids=true | all-gather | bytes 599040 | tf_op jit(solution)/shard_map/all_gather | solution.py:34
  354.2 0.1 broadcast_multiply_fusion
  354.3 0.6 copy.13
  354.9 0.5 reshape.13
  355.4 242.1 %all-reduce.2.cloned.1.call-done = f32[32,4608]{1,0:T(8,128)} async-done(((f32[32,4608]{1,0:T(8,128)}), f32[32,4608]{1,0:T(8,128)}) %all-reduce.2.cloned.1.call-update) | async-done | bytes 589840 | tf_op jit(solution)/shard_map/psum | solution.py:31
  597.5 2.0 bitcast_add_fusion
  599.6 0.7 constant_dynamic-slice_fusion
Async XLA Ops:
  7.2 24.9 %copy-start = (bf16[1,32,4608]{2,1,0:T(8,128)(2,1)S(1)}, bf16[1,32,4608]{2,1,0:T(8,128)(2,1)}, u32[]{:S(2)}) copy-start(bf16[1,32,4608]{2,1,0:T(8,128)(2,1)} %param.7) | copy-start | bytes 884740
  7.2 590.4 %all-reduce.2.cloned.1.call-start = ((), (), s32[]{:S(2)}) async-start(), calls=%async_computation | async-start | bytes 1179648 | tf_op jit(solution)/shard_map/psum | solution.py:31
  35.0 0.7 copy-start.1
  197.8 0.7 copy-start.2
Sparse Core Ops, SparseCore 0:
  35.1 562.3 all-reduce.1
where the time goes:
time: 607 us
  blocking collectives  340 us (56%)
  waiting for transfers between devices  242 us (40%)
  between operations  14.8 us (2%)
  other arithmetic  6.75 us (1%)
    psum x1, waiting for transfers between devices, body(): summed = lax.psum(stepped[0], 'rep')  242 us
    all_gather x1, blocking collectives, body(): lax.all_gather(anchor, 'rep', axis=1, tiled=True)  161 us
    all_gather x1, blocking collectives, body(): lax.all_gather(outer_momentum, 'rep', axis=1, tiled=True)  156 us
    psum x1, blocking collectives, body(): norm_square = lax.psum(partial_sum, 'fsdp')  22.4 us
  transfers between devices with their start and end apart: 1, of which 1 were waited for; matrix products, arithmetic and copies ran while one was open for 0% of the time, Pallas kernels for 0%

commit v1 on v0

v1 whole, which is shorter than its diff:
```python
import math

import jax
import jax.numpy as jnp
from jax import lax
from jax.sharding import Mesh
from jax.sharding import PartitionSpec as P

beta_one = 0.9
beta_two = 0.95
inner_rate = 0.01
weight_decay = 0.1
adam_eps = 1e-08
clip_rms = 0.5
outer_rate = 0.7
outer_beta = 0.9

FSDP = ("fz", "fc")
NEAR = ("zl", "x", "yl")
FAR = ("yh",)
REP = ("zl", "yh", "yl", "x")

gain = outer_rate * (1.0 + outer_beta)
keep = 1.0 - gain
drag = outer_rate * outer_beta * outer_beta


def exchange(value, axes):
    return lax.all_to_all(value, axes, 0, 0, tiled=True)


def spread(value, n):
    return jnp.broadcast_to(value[None], (n,) + value.shape)


def body(inner_weights, grads, first_moment, second_moment, anchor, outer_momentum):
    rows, width = grads.shape[1:]
    shards = lax.axis_size(FSDP)
    replicas = lax.axis_size(REP)
    near = lax.axis_size(NEAR)
    far = lax.axis_size(FAR)
    columns = anchor.shape[1]
    first_column = lax.axis_index(REP) * columns

    gradient = grads[0].astype(jnp.float32)
    partial_sum = jnp.sum(gradient * gradient)
    norm_square = jnp.sum(exchange(jnp.broadcast_to(partial_sum, (shards, 128)), FSDP)[:, 0])
    entries = rows * width * shards
    clip_factor = jnp.minimum(1.0, clip_rms * math.sqrt(entries) / jnp.sqrt(norm_square + 1e-06))
    clipped = gradient * clip_factor
    new_first = beta_one * first_moment[0] + (1.0 - beta_one) * clipped
    new_second = beta_two * second_moment[0] + (1.0 - beta_two) * clipped * clipped
    stepped = inner_weights[0] - inner_rate * (
        new_first / (jnp.sqrt(new_second) + adam_eps) + weight_decay * inner_weights[0]
    )
    part = (gain / replicas) * stepped
    own = lax.dynamic_slice_in_dim(part, first_column, columns, 1)
    part = lax.dynamic_update_slice_in_dim(
        part, own + keep * anchor - drag * outer_momentum, first_column, 1
    )
    groups = rows // 8
    cuts = near // groups
    blocks = part.reshape(groups, 8, cuts, width // cuts).transpose(0, 2, 1, 3)
    blocks = blocks.reshape(near, 8, width // cuts)
    mine = jnp.sum(exchange(blocks, NEAR), axis=0)
    mine = jnp.sum(exchange(spread(mine, far), FAR), axis=0)
    full = exchange(spread(mine, near), NEAR)
    new_params = full.reshape(groups, cuts, 8, width // cuts).transpose(0, 2, 1, 3).reshape(rows, width)
    own = lax.dynamic_slice_in_dim(new_params, first_column, columns, 1)
    mean = (own - keep * anchor + drag * outer_momentum) / gain
    new_momentum = outer_beta * outer_momentum + (anchor - mean)
    return (new_params, new_momentum, new_first[None], new_second[None])


def solution(mesh):
    fine = Mesh(
        mesh.devices.reshape(2, 4, 2, 4, 4, 2), ("zl", "yh", "yl", "x", "fz", "fc")
    )
    placed = (
        P(REP, FSDP, None),
        P(REP, FSDP, None),
        P(REP, FSDP, None),
        P(REP, FSDP, None),
        P(FSDP, REP),
        P(FSDP, REP),
    )
    return jax.shard_map(
        body,
        mesh=fine,
        in_specs=placed,
        out_specs=(
            P(FSDP, None),
            P(FSDP, REP),
            P(REP, FSDP, None),
            P(REP, FSDP, None),
        ),
        check_vma=False,
    )
```

time: 607 us -> 73.3 us (0.12)
  the two profiles are of different devices: /device:TPU:64 before, /device:TPU:8 now
where the time goes in v1:
time: 73.3 us; the launch traced here: 72.9 us
  blocking collectives  32.1 us (44%)
  waiting for transfers between devices  15 us (20%)
  starting transfers between devices  14.8 us (20%)
  other arithmetic  6.28 us (9%)
  local copies, waits for them, and re-layouts  3.35 us (5%)
  between operations  1.41 us (2%)
    all_to_all x2, blocking collectives, exchange(): return lax.all_to_all(value, axes, 0, 0, tiled=True)  32.1 us
    all_to_all x2, waiting for transfers between devices, exchange(): return lax.all_to_all(value, axes, 0, 0, tiled=True)  15 us
    all_to_all x2, starting transfers between devices, exchange(): return lax.all_to_all(value, axes, 0, 0, tiled=True)  14.8 us
    mul x1, other arithmetic, body(): part = gain / replicas * stepped  1.9 us
    reduce_sum x1, other arithmetic, body(): partial_sum = jnp.sum(gradient * gradient)  1.78 us
  transfers between devices with their start and end apart: 2, of which 2 were waited for; matrix products, arithmetic and copies ran while one was open for 2% of the time, Pallas kernels for 0%

profile of v1, /device:TPU:8, one launch (start us, length us, event | category | flops | bytes accessed | tf_op | source)
XLA Modules:
  0.0 72.9 jit_solution(16026469607594831991)
XLA Ops:
  0.6 0.0 copy-start
  0.6 1.8 %fusion.10 = f32[]{:T(128)} fusion(bf16[1,32,4608]{2,1,0:T(8,128)(2,1)} %param.7), kind=kLoop, calls=%fused_computation.14 | loop fusion | flops 442367 | bytes 294916 | tf_op jit(solution)/shard_map/reduce_sum | solution.py:46
  2.4 1.2 %broadcast_in_dim.6 = f32[8,1,128]{2,1,0:T(1,128)} broadcast(f32[]{:T(128)} %fusion.10), dimensions={} | broadcast | bytes 4100 | tf_op jit(solution)/shard_map/broadcast_in_dim | solution.py:47
  3.7 10.3 %all-to-all-start = ((f32[8,1,128]{2,1,0:T(1,128)}), f32[8,1,128]{2,1,0:T(1,128)S(1)}, u32[]{:S(2)}, u32[]{:S(2)}) async-start(f32[8,1,128]{2,1,0:T(1,128)} %broadcast_in_dim.6), calls=%async_computation | async-start | bytes 8192 | tf_op jit(solution)/shard_map/all_to_all | solution.py:29
  14.0 7.6 %all-to-all-done = f32[8,1,128]{2,1,0:T(1,128)S(1)} async-done(((f32[8,1,128]{2,1,0:T(1,128)}), f32[8,1,128]{2,1,0:T(1,128)S(1)}, u32[]{:S(2)}, u32[]{:S(2)}) %all-to-all-start) | async-done | bytes 4128 | tf_op jit(solution)/shard_map/all_to_all | solution.py:29
  21.6 0.6 slice_reduce_fusion
  22.9 0.0 copy-done
  22.9 0.0 copy-start.3
  22.9 0.0 copy-start.4
  22.9 1.9 %fusion.8 = f32[32,4608]{1,0:T(8,128)S(1)} fusion(bf16[1,32,4608]{2,1,0:T(8,128)(2,1)S(1)} %copy-done, f32[1,32,4608]{2,1,0:T(8,128)} %param.6, f32[1,32,4608]{2,1,0:T(8,128)} %param.9, f32[1,32,4608]{2,1,0:T(8,128)} %param.8, f32[]{:T(128)S(6)} %min_shard_map.3), kind=kLoop, calls=%fused_computation.12 | loop fusion | flops 2359296 | bytes 2654212 | tf_op jit(solution)/shard_map/mul | solution.py:56
  24.8 0.0 copy-done.3
  24.8 0.0 copy-done.4
  24.8 0.1 add_subtract_fusion
  24.9 0.4 dynamic_update_slice.3
  25.3 16.8 %all_to_all.24 = f32[16,8,1152]{2,1,0:T(8,128)S(1)} all-to-all(f32[16,8,1152]{2,1,0:T(8,128)S(1)} %bitcast.48), channel_id=1, replica_groups=mesh['zl'=2,'yh'=4,'yl'=2,'x'=4,'fz'=4,'fc'=2] {'zl','x','yl'}, dimensions={0} | all-to-all | bytes 1179648 | tf_op jit(solution)/shard_map/all_to_all | solution.py:29
  42.2 15.2 %all_to_all.25 = f32[4,8,1152]{2,1,0:T(8,128)S(1)} all-to-all(f32[4,8,1152]{2,1,0:T(8,128)S(1)} %broadcast_in_dim.7), channel_id=1, replica_groups=mesh['zl'=2,'yh'=4,'yl'=2,'x'=4,'fz'=4,'fc'=2] {'yh'}, dimensions={0} | all-to-all | bytes 294912 | tf_op jit(solution)/shard_map/all_to_all | solution.py:29
  57.5 0.9 %broadcast_in_dim.8 = f32[16,8,1152]{2,1,0:T(8,128)} broadcast(f32[8,1152]{1,0:T(8,128)S(1)} %reduce_sum.39), dimensions={1,2} | broadcast | bytes 626688 | tf_op jit(solution)/shard_map/broadcast_in_dim | solution.py:33
  58.3 0.0 copy-start.1
  58.3 0.0 copy-start.2
  58.3 4.5 %all-to-all-start.3 = ((f32[16,8,1152]{2,1,0:T(8,128)}), f32[16,8,1152]{2,1,0:T(8,128)S(1)}, u32[]{:S(2)}, u32[]{:S(2)}) async-start(f32[16,8,1152]{2,1,0:T(8,128)} %broadcast_in_dim.8), calls=%async_computation.3 | async-start | bytes 1179648 | tf_op jit(solution)/shard_map/all_to_all | solution.py:29
  62.8 0.0 copy-done.1
  62.8 0.0 copy-done.2
  62.8 1.2 %fusion.14 = (f32[1,32,4608]{2,1,0:T(8,128)}, f32[1,32,4608]{2,1,0:T(8,128)}) fusion(bf16[1,32,4608]{2,1,0:T(8,128)(2,1)S(1)} %copy-done, f32[1,32,4608]{2,1,0:T(8,128)S(1)} %copy-done.1, f32[]{:T(128)S(6)} %min_shard_map.3, f32[1,32,4608]{2,1,0:T(8,128)S(1)} %copy-done.2), kind=kLoop, calls=%fused_computation.18 | loop fusion | flops 1327104 | bytes 2654212 | tf_op jit(solution)/shard_map/add | solution.py:52
  64.0 7.4 %all-to-all-done.3 = f32[16,8,1152]{2,1,0:T(8,128)S(1)} async-done(((f32[16,8,1152]{2,1,0:T(8,128)}), f32[16,8,1152]{2,1,0:T(8,128)S(1)}, u32[]{:S(2)}, u32[]{:S(2)}) %all-to-all-start.3) | async-done | bytes 589856 | tf_op jit(solution)/shard_map/all_to_all | solution.py:29
  71.4 0.7 subtract_add_fusion
  72.1 0.8 %copy.14 = f32[32,4608]{1,0:T(8,128)} copy(f32[32,4608]{1,0:T(8,128)S(1)} %bitcast.47) | data formatting | bytes 1179648
  (3 shorter events, 0.1 us)
Async XLA Ops:
  0.6 22.2 %copy-start = (bf16[1,32,4608]{2,1,0:T(8,128)(2,1)S(1)}, bf16[1,32,4608]{2,1,0:T(8,128)(2,1)}, u32[]{:S(2)}) copy-start(bf16[1,32,4608]{2,1,0:T(8,128)(2,1)} %param.7) | copy-start | bytes 884740
  3.7 17.9 %all-to-all-start = ((f32[8,1,128]{2,1,0:T(1,128)}), f32[8,1,128]{2,1,0:T(1,128)S(1)}, u32[]{:S(2)}, u32[]{:S(2)}) async-start(f32[8,1,128]{2,1,0:T(1,128)} %broadcast_in_dim.6), calls=%async_computation | async-start | bytes 8192 | tf_op jit(solution)/shard_map/all_to_all | solution.py:29
  22.9 1.9 %copy-start.3 = (f32[32,72]{1,0:T(8,128)S(1)}, f32[32,72]{1,0:T(8,128)}, u32[]{:S(2)}) copy-start(f32[32,72]{1,0:T(8,128)} %param.11) | copy-start | bytes 27652
  22.9 1.9 %copy-start.4 = (f32[32,72]{1,0:T(8,128)S(1)}, f32[32,72]{1,0:T(8,128)}, u32[]{:S(2)}) copy-start(f32[32,72]{1,0:T(8,128)} %param.10) | copy-start | bytes 27652
  58.3 4.5 %copy-start.1 = (f32[1,32,4608]{2,1,0:T(8,128)S(1)}, f32[1,32,4608]{2,1,0:T(8,128)}, u32[]{:S(2)}) copy-start(f32[1,32,4608]{2,1,0:T(8,128)} %param.9) | copy-start | bytes 1769476
  58.3 4.5 %copy-start.2 = (f32[1,32,4608]{2,1,0:T(8,128)S(1)}, f32[1,32,4608]{2,1,0:T(8,128)}, u32[]{:S(2)}) copy-start(f32[1,32,4608]{2,1,0:T(8,128)} %param.8) | copy-start | bytes 1769476
  58.3 13.1 %all-to-all-start.3 = ((f32[16,8,1152]{2,1,0:T(8,128)}), f32[16,8,1152]{2,1,0:T(8,128)S(1)}, u32[]{:S(2)}, u32[]{:S(2)}) async-start(f32[16,8,1152]{2,1,0:T(8,128)} %broadcast_in_dim.8), calls=%async_computation.3 | async-start | bytes 1179648 | tf_op jit(solution)/shard_map/all_to_all | solution.py:29

commit v2 on v1

v2 whole, which is shorter than its diff:
```python
import math

import jax
import jax.numpy as jnp
from jax import lax
from jax.experimental import pallas as pl
from jax.experimental.pallas import tpu as pltpu
from jax.sharding import Mesh
from jax.sharding import PartitionSpec as P

beta_one = 0.9
beta_two = 0.95
inner_rate = 0.01
weight_decay = 0.1
adam_eps = 1e-08
clip_rms = 0.5
outer_rate = 0.7
outer_beta = 0.9

FSDP = ("fz", "fc")
NEAR = ("zl", "x", "yl")
FAR = ("yh",)
REP = ("zl", "yh", "yl", "x")

gain = outer_rate * (1.0 + outer_beta)
keep = 1.0 - gain
drag = outer_rate * outer_beta * outer_beta

SUB, LANE = 8, 128
PIECES = 2
SMALL = pltpu.CompilerParams(vmem_limit_bytes=4 * 2**20)
VMEM = pl.BlockSpec(memory_space=pltpu.VMEM)
ANY = pl.BlockSpec(memory_space=pl.ANY)
f32 = jnp.float32


def exchange(value, axes):
    return lax.all_to_all(value, axes, 0, 0, tiled=True)


def in_hbm(value):
    return pltpu.with_memory_space_constraint(value, pltpu.HBM)


def square_kernel(grads_ref, parts_ref, held_ref, arrived):
    rows, width = grads_ref.shape[1:]
    step = rows // PIECES
    copies = []
    for i in range(PIECES):
        here = (0, slice(i * step, (i + 1) * step))
        copies.append(pltpu.make_async_copy(grads_ref.at[here], held_ref.at[here], arrived.at[i]))
        copies[-1].start()
    total = jnp.zeros((step, LANE), f32)
    for i in range(PIECES):
        copies[i].wait()
        for at in range(0, width, LANE):
            tile = held_ref[0, i * step : (i + 1) * step, at : at + LANE].astype(f32)
            total += tile * tile
    tile = sum(total[at : at + SUB] for at in range(0, step, SUB))
    parts_ref[...] = jnp.broadcast_to(tile[None], parts_ref.shape)


def first_column(columns):
    index = 0
    for axis in REP:
        index = index * lax.axis_size(axis) + lax.axis_index(axis)
    return index * columns


def window(first, width):
    tile = jnp.minimum(first // LANE, width // LANE - 2)
    start = pl.multiple_of(tile * LANE, LANE)
    return start, first - start


def hold_kernel(
    scale, weights_ref, first_ref, second_ref, anchor_ref, outer_ref, base_ref, old_first_ref, old_second_ref, arrived
):
    copies = []
    pairs = ((weights_ref, base_ref), (first_ref, old_first_ref), (second_ref, old_second_ref))
    for i, (given, held) in enumerate(pairs):
        copies.append(pltpu.make_async_copy(given, held, arrived.at[i]))
        copies[-1].start()
    rows, width = base_ref.shape[1:]
    mine = keep * anchor_ref[...] - drag * outer_ref[...]
    columns = mine.shape[1]
    start, shift = window(first_column(columns), width)
    mine = jnp.concatenate([mine, jnp.zeros((rows, 2 * LANE - columns), f32)], axis=1)
    mine = pltpu.roll(mine, shift, 1)
    copies[0].wait()
    base_ref[...] = (scale * (1.0 - inner_rate * weight_decay)) * base_ref[...]
    base_ref[0, :, pl.ds(start, 2 * LANE)] += mine
    copies[1].wait()
    old_first_ref[...] = beta_one * old_first_ref[...]
    copies[2].wait()
    old_second_ref[...] = beta_two * old_second_ref[...]


def step_kernel(
    scale, entries, parts_ref, grads_ref, base_ref, old_first_ref, old_second_ref, blocks_ref, new_first_ref, new_second_ref
):
    rows, width = base_ref.shape[1:]
    cut = blocks_ref.shape[2]
    cuts = width // cut
    norm_square = jnp.sum(parts_ref[...])
    clip_factor = jnp.minimum(
        1.0, clip_rms * math.sqrt(entries) * lax.rsqrt(jnp.full((SUB, LANE), norm_square + 1e-06))
    )
    clip_row = clip_factor[:1, :1]
    for top in range(0, rows, 2 * SUB):
        for at in range(cuts):
            here = (0, slice(top, top + 2 * SUB), slice(at * cut, (at + 1) * cut))
            clipped = grads_ref[here].astype(f32) * clip_row
            new_first = old_first_ref[here] + (1.0 - beta_one) * clipped
            new_second = old_second_ref[here] + (1.0 - beta_two) * clipped * clipped
            new_first_ref[here] = new_first
            new_second_ref[here] = new_second
            block = base_ref[here] - (scale * inner_rate) * (new_first / (jnp.sqrt(new_second) + adam_eps))
            for half in range(2):
                blocks_ref[(top // SUB + half) * cuts + at] = block[half * SUB : (half + 1) * SUB]


def sum_kernel(given_ref, sums_ref):
    total = given_ref[0]
    for at in range(1, given_ref.shape[0]):
        total += given_ref[at]
    sums_ref[...] = jnp.broadcast_to(total[None], sums_ref.shape)


def sum_spread(given, n):
    return pl.pallas_call(
        sum_kernel,
        out_shape=pltpu.VMEM((n,) + given.shape[1:], f32),
        in_specs=[VMEM],
        out_specs=VMEM,
        compiler_params=SMALL,
        name="sum",
    )(given)


def copies_kernel(given_ref, out_ref, total_ref, done):
    total = given_ref[0]
    for at in range(1, given_ref.shape[0]):
        total += given_ref[at]
    total_ref[...] = total
    copies = [pltpu.make_async_copy(total_ref, out_ref.at[at], done.at[at]) for at in range(out_ref.shape[0])]
    for copy in copies:
        copy.start()
    for copy in copies:
        copy.wait()


def sum_copies(given, n):
    return pl.pallas_call(
        copies_kernel,
        out_shape=jax.ShapeDtypeStruct((n,) + given.shape[1:], f32),
        in_specs=[VMEM],
        out_specs=ANY,
        scratch_shapes=[pltpu.VMEM(given.shape[1:], f32), pltpu.SemaphoreType.DMA((n,))],
        compiler_params=SMALL,
        name="copies",
    )(given)


def outer_kernel(full_ref, anchor_ref, outer_ref, params_ref, momentum_ref, own_ref, done):
    copies = []
    for at in range(full_ref.shape[0] // SUB):
        here = slice(at * SUB, (at + 1) * SUB)
        copies.append(pltpu.make_async_copy(full_ref.at[here], params_ref.at[here], done.at[at]))
        copies[-1].start()
    columns = anchor_ref.shape[1]
    start, shift = window(first_column(columns), full_ref.shape[1])
    near = full_ref[:, pl.ds(start, 2 * LANE)]
    own = pltpu.roll(near, 2 * LANE - shift, 1)[:, :columns]
    mean = (own - keep * anchor_ref[...] + drag * outer_ref[...]) / gain
    own_ref[...] = outer_beta * outer_ref[...] + (anchor_ref[...] - mean)
    copies.append(pltpu.make_async_copy(own_ref, momentum_ref, done.at[len(copies)]))
    copies[-1].start()
    for copy in copies:
        copy.wait()


def body(inner_weights, grads, first_moment, second_moment, anchor, outer_momentum):
    rows, width = grads.shape[1:]
    shards = lax.axis_size(FSDP)
    replicas = lax.axis_size(REP)
    near = lax.axis_size(NEAR)
    far = lax.axis_size(FAR)
    columns = anchor.shape[1]
    groups = rows // SUB
    cuts = near // groups
    scale = gain / replicas

    parts, grads = pl.pallas_call(
        square_kernel,
        out_shape=(pltpu.VMEM((shards, SUB, LANE), f32), pltpu.VMEM(grads.shape, grads.dtype)),
        in_specs=[ANY],
        out_specs=(VMEM, VMEM),
        scratch_shapes=[pltpu.SemaphoreType.DMA((PIECES,))],
        compiler_params=SMALL,
        name="square",
    )(in_hbm(grads))
    parts = exchange(parts, FSDP)

    def hold(*refs):
        hold_kernel(scale, *refs)

    held = pl.pallas_call(
        hold,
        out_shape=(pltpu.VMEM((1, rows, width), f32),) * 3,
        in_specs=[ANY, ANY, ANY, VMEM, VMEM],
        out_specs=(VMEM,) * 3,
        scratch_shapes=[pltpu.SemaphoreType.DMA((3,))],
        compiler_params=SMALL,
        cost_estimate=pl.CostEstimate(flops=10**7, bytes_accessed=10**7, transcendentals=0),
        name="hold",
    )(in_hbm(inner_weights), in_hbm(first_moment), in_hbm(second_moment), anchor, outer_momentum)

    def step(*refs):
        step_kernel(scale, rows * width * shards, *refs)

    blocks, new_first, new_second = pl.pallas_call(
        step,
        out_shape=(
            pltpu.VMEM((near, SUB, width // cuts), f32),
            pltpu.VMEM((1, rows, width), f32),
            pltpu.VMEM((1, rows, width), f32),
        ),
        in_specs=[VMEM] * 5,
        out_specs=(VMEM,) * 3,
        input_output_aliases={3: 1, 4: 2},
        compiler_params=SMALL,
        name="step",
    )(parts, grads, *held)
    mine = sum_spread(exchange(blocks, NEAR), far)
    mine = sum_copies(exchange(mine, FAR), near)
    full = exchange(mine, NEAR)
    full = full.reshape(groups, cuts, SUB, width // cuts).transpose(0, 2, 1, 3).reshape(rows, width)
    new_params, new_momentum = pl.pallas_call(
        outer_kernel,
        out_shape=(jax.ShapeDtypeStruct((rows, width), f32), jax.ShapeDtypeStruct((rows, columns), f32)),
        in_specs=[VMEM] * 3,
        out_specs=(ANY, ANY),
        scratch_shapes=[pltpu.VMEM((rows, columns), f32), pltpu.SemaphoreType.DMA((groups + 1,))],
        compiler_params=SMALL,
        name="outer",
    )(full, anchor, outer_momentum)
    return (new_params, new_momentum, new_first, new_second)


def solution(mesh):
    fine = Mesh(
        mesh.devices.reshape(2, 4, 2, 4, 4, 2), ("zl", "yh", "yl", "x", "fz", "fc")
    )
    placed = (
        P(REP, FSDP, None),
        P(REP, FSDP, None),
        P(REP, FSDP, None),
        P(REP, FSDP, None),
        P(FSDP, REP),
        P(FSDP, REP),
    )
    return jax.shard_map(
        body,
        mesh=fine,
        in_specs=placed,
        out_specs=(
            P(FSDP, None),
            P(FSDP, REP),
            P(REP, FSDP, None),
            P(REP, FSDP, None),
        ),
        check_vma=False,
    )
```

time: 73.3 us -> 68.4 us (0.933)
  other arithmetic: 6.28 us -> 0 us
  Pallas kernels: 0 us -> 5.52 us
  local copies, waits for them, and re-layouts: 3.35 us -> 1.64 us
  waiting for transfers between devices: 15 us -> 13.4 us
    pallas_call x0 -> x6, Pallas kernels: none -> 5.52 us  [the longest x1 1.66 us: body(): pl.pallas_call(square_kernel, out_shape=(pltpu.VMEM((shards, SUB, LANE),...]
    reduce_sum x4 -> x0, other arithmetic: 2.43 us -> none  [the longest x1 1.78 us: body(): partial_sum = jnp.sum(gradient * gradient)]
    broadcast_in_dim x3 -> x0, local copies, waits for them, and re-layouts: 2.1 us -> none  [the longest x1 1.24 us: body(): jnp.broadcast_to(partial_sum, (shards, 128))]
    mul x1 -> x0, other arithmetic: 1.9 us -> none  [body(): part = gain / replicas * stepped]
    add x2 -> x0, other arithmetic: 1.87 us -> none  [the longest x1 1.19 us: body(): beta_two * second_moment[0] + (1.0 - beta_two) * clipped * clipped]
    all_to_all x2, waiting for transfers between devices: 15 us -> 13.4 us  [exchange(): return lax.all_to_all(value, axes, 0, 0, tiled=True)]
    unnamed x11 -> x6, local copies, waits for them, and re-layouts: 0.84 us -> 1.64 us
  transfers between devices with their start and end apart: 2 -> 2, of which waited for: 2 -> 2; matrix products, arithmetic and copies ran while one was open for 2% -> 2% of each run, Pallas kernels for 0% -> 2%
where the time goes in v2:
time: 68.4 us; the launch traced here: 67.9 us
  blocking collectives  32 us (47%)
  starting transfers between devices  14.7 us (21%)
  waiting for transfers between devices  13.4 us (20%)
  Pallas kernels  5.52 us (8%)
  local copies, waits for them, and re-layouts  1.64 us (2%)
  between operations  0.69 us (1%)
    all_to_all x2, blocking collectives, exchange(): return lax.all_to_all(value, axes, 0, 0, tiled=True)  32 us
    all_to_all x2, starting transfers between devices, exchange(): return lax.all_to_all(value, axes, 0, 0, tiled=True)  14.7 us
    all_to_all x2, waiting for transfers between devices, exchange(): return lax.all_to_all(value, axes, 0, 0, tiled=True)  13.4 us
    pallas_call x1, Pallas kernels, body(): pl.pallas_call(square_kernel, out_shape=(pltpu.VMEM((shards, SUB, LANE),...  1.66 us
    unnamed x6, local copies, waits for them, and re-layouts  1.64 us
    pallas_call x1, Pallas kernels, body(): pl.pallas_call(hold, out_shape=(pltpu.VMEM((1, rows, width), f32),) * 3,...  1.52 us
  transfers between devices with their start and end apart: 2, of which 2 were waited for; matrix products, arithmetic and copies ran while one was open for 2% of the time, Pallas kernels for 2%

profile of v2, /device:TPU:8, one launch (start us, length us, event | category | flops | bytes accessed | tf_op | source)
XLA Modules:
  0.0 67.9 jit_solution(6895848815644914068)
XLA Ops:
  0.6 1.7 %square.1 = (f32[8,8,128]{2,1,0:T(8,128)}, bf16[1,32,4608]{2,1,0:T(8,128)(2,1)S(1)}) custom-call(bf16[1,32,4608]{2,1,0:T(8,128)(2,1)} %grads_ref.1), custom_call_target="tpu_custom_call" | custom-call | tf_op jit(solution)/shard_map/square/pallas_call | solution.py:194
  2.3 0.0 copy-start
  2.3 0.0 copy-start.1
  2.3 10.3 %all-to-all-start = ((f32[8,8,128]{2,1,0:T(8,128)}), f32[8,8,128]{2,1,0:T(8,128)S(1)}, u32[]{:S(2)}, u32[]{:S(2)}) async-start(f32[8,8,128]{2,1,0:T(8,128)} %get-tuple-element.14), calls=%async_computation | async-start | bytes 65536 | tf_op jit(solution)/shard_map/all_to_all | solution.py:38
  12.6 0.0 copy-done
  12.6 0.0 copy-done.1
  12.7 1.5 %hold.1 = (f32[1,32,4608]{2,1,0:T(8,128)S(1)}, f32[1,32,4608]{2,1,0:T(8,128)S(1)}, f32[1,32,4608]{2,1,0:T(8,128)S(1)}) custom-call(f32[1,32,4608]{2,1,0:T(8,128)} %refs_0_.1, f32[1,32,4608]{2,1,0:T(8,128)} %refs_1_.1, f32[1,32,4608]{2,1,0:T(8,128)} %refs_2_.1, f32[32,72]{1,0:T(8,128)S(1)} %copy-done, f32[32,72]{1,0:T(8,128)S(1)} %copy-done.1), custom_call_target="tpu_custom_call" | custom-call | flops 10000000 | bytes 10000000 | tf_op jit(solution)/shard_map/hold/pallas_call | solution.py:208
  14.2 6.5 %all-to-all-done.refs_0_ = f32[8,8,128]{2,1,0:T(8,128)S(1)} async-done(((f32[8,8,128]{2,1,0:T(8,128)}), f32[8,8,128]{2,1,0:T(8,128)S(1)}, u32[]{:S(2)}, u32[]{:S(2)}) %all-to-all-start) | async-done | bytes 32800 | tf_op jit(solution)/shard_map/all_to_all | solution.py:38
  20.7 0.5 step.1
  21.2 16.7 %all_to_all.20.given_ref = f32[16,8,1152]{2,1,0:T(8,128)S(1)} all-to-all(f32[16,8,1152]{2,1,0:T(8,128)S(1)} %get-tuple-element.19), channel_id=1, replica_groups=mesh['zl'=2,'yh'=4,'yl'=2,'x'=4,'fz'=4,'fc'=2] {'zl','x','yl'}, dimensions={0} | all-to-all | bytes 1179648 | tf_op jit(solution)/shard_map/all_to_all | solution.py:38
  37.9 15.2 %all_to_all.21.given_ref = f32[4,8,1152]{2,1,0:T(8,128)S(1)} all-to-all(f32[4,8,1152]{2,1,0:T(8,128)S(1)} %sum.1), channel_id=1, replica_groups=mesh['zl'=2,'yh'=4,'yl'=2,'x'=4,'fz'=4,'fc'=2] {'yh'}, dimensions={0} | all-to-all | bytes 294912 | tf_op jit(solution)/shard_map/all_to_all | solution.py:38
  53.2 0.9 %copies.1 = f32[16,8,1152]{2,1,0:T(8,128)} custom-call(f32[4,8,1152]{2,1,0:T(8,128)S(1)} %all_to_all.21.given_ref), custom_call_target="tpu_custom_call" | custom-call | tf_op jit(solution)/shard_map/copies/pallas_call | solution.py:154
  54.1 4.4 %all-to-all-start.3 = ((f32[16,8,1152]{2,1,0:T(8,128)}), f32[16,8,1152]{2,1,0:T(8,128)S(1)}, u32[]{:S(2)}, u32[]{:S(2)}) async-start(f32[16,8,1152]{2,1,0:T(8,128)} %copies.1), calls=%async_computation.3 | async-start | bytes 1179648 | tf_op jit(solution)/shard_map/all_to_all | solution.py:38
  58.5 0.8 %copy.14 = f32[1,32,4608]{2,1,0:T(8,128)} copy(f32[1,32,4608]{2,1,0:T(8,128)S(1)} %get-tuple-element.26) | data formatting | bytes 1179648
  59.3 0.8 %copy.15 = f32[1,32,4608]{2,1,0:T(8,128)} copy(f32[1,32,4608]{2,1,0:T(8,128)S(1)} %get-tuple-element.27) | data formatting | bytes 1179648
  60.1 6.9 %all-to-all-done.3 = f32[16,8,1152]{2,1,0:T(8,128)S(1)} async-done(((f32[16,8,1152]{2,1,0:T(8,128)}), f32[16,8,1152]{2,1,0:T(8,128)S(1)}, u32[]{:S(2)}, u32[]{:S(2)}) %all-to-all-start.3) | async-done | bytes 589856 | tf_op jit(solution)/shard_map/all_to_all | solution.py:38
  67.1 0.9 %outer.1 = (f32[32,4608]{1,0:T(8,128)}, f32[32,72]{1,0:T(8,128)}) custom-call(f32[32,4608]{1,0:T(8,128)S(1)} %bitcast.5, f32[32,72]{1,0:T(8,128)S(1)} %copy-done, f32[32,72]{1,0:T(8,128)S(1)} %copy-done.1), custom_call_target="tpu_custom_call" | custom-call | tf_op jit(solution)/shard_map/outer/pallas_call | solution.py:239
  (1 shorter events, 0.0 us)
Async XLA Ops:
  2.3 10.3 %copy-start = (f32[32,72]{1,0:T(8,128)S(1)}, f32[32,72]{1,0:T(8,128)}, u32[]{:S(2)}) copy-start(f32[32,72]{1,0:T(8,128)} %anchor_ref.1) | copy-start | bytes 27652
  2.3 10.3 %copy-start.1 = (f32[32,72]{1,0:T(8,128)S(1)}, f32[32,72]{1,0:T(8,128)}, u32[]{:S(2)}) copy-start(f32[32,72]{1,0:T(8,128)} %outer_ref.1) | copy-start | bytes 27652
  2.3 18.3 %all-to-all-start = ((f32[8,8,128]{2,1,0:T(8,128)}), f32[8,8,128]{2,1,0:T(8,128)S(1)}, u32[]{:S(2)}, u32[]{:S(2)}) async-start(f32[8,8,128]{2,1,0:T(8,128)} %get-tuple-element.14), calls=%async_computation | async-start | bytes 65536 | tf_op jit(solution)/shard_map/all_to_all | solution.py:38
  54.1 12.9 %all-to-all-start.3 = ((f32[16,8,1152]{2,1,0:T(8,128)}), f32[16,8,1152]{2,1,0:T(8,128)S(1)}, u32[]{:S(2)}, u32[]{:S(2)}) async-start(f32[16,8,1152]{2,1,0:T(8,128)} %copies.1), calls=%async_computation.3 | async-start | bytes 1179648 | tf_op jit(solution)/shard_map/all_to_all | solution.py:38

commit v3 on v2

--- a/solution.py
+++ b/solution.py
@@ -27,7 +27,7 @@
 drag = outer_rate * outer_beta * outer_beta
 
 SUB, LANE = 8, 128
-PIECES = 2
+PIECES = 4
 SMALL = pltpu.CompilerParams(vmem_limit_bytes=4 * 2**20)
 VMEM = pl.BlockSpec(memory_space=pltpu.VMEM)
 ANY = pl.BlockSpec(memory_space=pl.ANY)
@@ -44,19 +44,21 @@
 
 def square_kernel(grads_ref, parts_ref, held_ref, arrived):
     rows, width = grads_ref.shape[1:]
-    step = rows // PIECES
+    step = 2 * SUB
+    cut = width // PIECES
+    pieces = [(top, at) for top in range(0, rows, step) for at in range(0, width, cut)]
     copies = []
-    for i in range(PIECES):
-        here = (0, slice(i * step, (i + 1) * step))
+    for i, (top, at) in enumerate(pieces):
+        here = (0, slice(top, top + step), slice(at, at + cut))
         copies.append(pltpu.make_async_copy(grads_ref.at[here], held_ref.at[here], arrived.at[i]))
         copies[-1].start()
     total = jnp.zeros((step, LANE), f32)
-    for i in range(PIECES):
-        copies[i].wait()
-        for at in range(0, width, LANE):
-            tile = held_ref[0, i * step : (i + 1) * step, at : at + LANE].astype(f32)
+    for copy, (top, at) in zip(copies, pieces):
+        copy.wait()
+        for lane in range(at, at + cut, LANE):
+            tile = held_ref[0, top : top + step, lane : lane + LANE].astype(f32)
             total += tile * tile
-    tile = sum(total[at : at + SUB] for at in range(0, step, SUB))
+    tile = total[:SUB] + total[SUB:]
     parts_ref[...] = jnp.broadcast_to(tile[None], parts_ref.shape)
 
 
@@ -120,25 +122,27 @@
                 blocks_ref[(top // SUB + half) * cuts + at] = block[half * SUB : (half + 1) * SUB]
 
 
-def sum_kernel(given_ref, sums_ref):
+def sum_kernel(given_ref, *refs):
+    sums_ref = refs[-1]
     total = given_ref[0]
     for at in range(1, given_ref.shape[0]):
         total += given_ref[at]
     sums_ref[...] = jnp.broadcast_to(total[None], sums_ref.shape)
 
 
-def sum_spread(given, n):
+def sum_spread(given, n, *after):
     return pl.pallas_call(
         sum_kernel,
         out_shape=pltpu.VMEM((n,) + given.shape[1:], f32),
-        in_specs=[VMEM],
+        in_specs=[VMEM] * (1 + len(after)),
         out_specs=VMEM,
         compiler_params=SMALL,
         name="sum",
-    )(given)
-
-
-def copies_kernel(given_ref, out_ref, total_ref, done):
+    )(given, *after)
+
+
+def copies_kernel(given_ref, *refs):
+    out_ref, total_ref, done = refs[-3:]
     total = given_ref[0]
     for at in range(1, given_ref.shape[0]):
         total += given_ref[at]
@@ -160,6 +164,31 @@
         compiler_params=SMALL,
         name="copies",
     )(given)
+
+
+def write_kernel(first_ref, second_ref, _after, new_first_ref, new_second_ref, mark_ref, done):
+    copies = []
+    for given, out in ((first_ref, new_first_ref), (second_ref, new_second_ref)):
+        for at in range(0, given.shape[1], SUB):
+            here = (0, slice(at, at + SUB))
+            copies.append(pltpu.make_async_copy(given.at[here], out.at[here], done.at[len(copies)]))
+            copies[-1].start()
+    mark_ref[...] = jnp.zeros(mark_ref.shape, f32)
+    for copy in copies:
+        copy.wait()
+
+
+def write_moments(first, second, after):
+    return pl.pallas_call(
+        write_kernel,
+        out_shape=(jax.ShapeDtypeStruct(first.shape, f32),) * 2 + (pltpu.VMEM((SUB, LANE), f32),),
+        in_specs=[VMEM, VMEM, ANY],
+        out_specs=(ANY, ANY, VMEM),
+        scratch_shapes=[pltpu.SemaphoreType.DMA((2 * first.shape[1] // SUB,))],
+        compiler_params=SMALL,
+        cost_estimate=pl.CostEstimate(flops=10**6, bytes_accessed=4 * 10**6, transcendentals=0),
+        name="write",
+    )(first, second, after)
 
 
 def outer_kernel(full_ref, anchor_ref, outer_ref, params_ref, momentum_ref, own_ref, done):
@@ -196,7 +225,7 @@
         out_shape=(pltpu.VMEM((shards, SUB, LANE), f32), pltpu.VMEM(grads.shape, grads.dtype)),
         in_specs=[ANY],
         out_specs=(VMEM, VMEM),
-        scratch_shapes=[pltpu.SemaphoreType.DMA((PIECES,))],
+        scratch_shapes=[pltpu.SemaphoreType.DMA((rows // (2 * SUB) * PIECES,))],
         compiler_params=SMALL,
         name="square",
     )(in_hbm(grads))
@@ -232,8 +261,9 @@
         compiler_params=SMALL,
         name="step",
     )(parts, grads, *held)
-    mine = sum_spread(exchange(blocks, NEAR), far)
-    mine = sum_copies(exchange(mine, FAR), near)
+    mine = sum_copies(exchange(blocks, NEAR), far)
+    new_first, new_second, mark = write_moments(new_first, new_second, mine)
+    mine = sum_spread(exchange(mine, FAR), near, mark)
     full = exchange(mine, NEAR)
     full = full.reshape(groups, cuts, SUB, width // cuts).transpose(0, 2, 1, 3).reshape(rows, width)
     new_params, new_momentum = pl.pallas_call(

time: 68.4 us -> 67.5 us (0.987)
  the two profiles are of different devices: /device:TPU:8 before, /device:TPU:2 now
where the time goes in v3:
time: 67.5 us; the launch traced here: 67 us
  blocking collectives  29.2 us (43%)
  starting transfers between devices  16.5 us (24%)
  waiting for transfers between devices  14.3 us (21%)
  Pallas kernels  6.31 us (9%)
  between operations  0.7 us (1%)
    all_to_all x2, blocking collectives, exchange(): return lax.all_to_all(value, axes, 0, 0, tiled=True)  29.2 us
    all_to_all x2, starting transfers between devices, exchange(): return lax.all_to_all(value, axes, 0, 0, tiled=True)  16.5 us
    all_to_all x2, waiting for transfers between devices, exchange(): return lax.all_to_all(value, axes, 0, 0, tiled=True)  14.3 us
    pallas_call x1, Pallas kernels, body(): pl.pallas_call(square_kernel, out_shape=(pltpu.VMEM((shards, SUB, LANE),...  1.6 us
    pallas_call x1, Pallas kernels, body(): pl.pallas_call(hold, out_shape=(pltpu.VMEM((1, rows, width), f32),) * 3,...  1.52 us
  transfers between devices with their start and end apart: 2, of which 2 were waited for; matrix products, arithmetic and copies ran while one was open for 0% of the time, Pallas kernels for 4%

profile of v3, /device:TPU:2, one launch (start us, length us, event | category | flops | bytes accessed | tf_op | source)
XLA Modules:
  0.0 67.0 jit_solution(6858754920024810911)
XLA Ops:
  0.6 1.6 %square.1 = (f32[8,8,128]{2,1,0:T(8,128)}, bf16[1,32,4608]{2,1,0:T(8,128)(2,1)S(1)}) custom-call(bf16[1,32,4608]{2,1,0:T(8,128)(2,1)} %grads_ref.1), custom_call_target="tpu_custom_call" | custom-call | tf_op jit(solution)/shard_map/square/pallas_call | solution.py:223
  2.2 0.0 copy-start
  2.2 0.0 copy-start.1
  2.3 10.3 %all-to-all-start = ((f32[8,8,128]{2,1,0:T(8,128)}), f32[8,8,128]{2,1,0:T(8,128)S(1)}, u32[]{:S(2)}, u32[]{:S(2)}) async-start(f32[8,8,128]{2,1,0:T(8,128)} %get-tuple-element.17), calls=%async_computation | async-start | bytes 65536 | tf_op jit(solution)/shard_map/all_to_all | solution.py:38
  12.6 0.0 copy-done
  12.6 0.0 copy-done.1
  12.6 1.5 %hold.1 = (f32[1,32,4608]{2,1,0:T(8,128)S(1)}, f32[1,32,4608]{2,1,0:T(8,128)S(1)}, f32[1,32,4608]{2,1,0:T(8,128)S(1)}) custom-call(f32[1,32,4608]{2,1,0:T(8,128)} %refs_0_.1, f32[1,32,4608]{2,1,0:T(8,128)} %refs_1_.1, f32[1,32,4608]{2,1,0:T(8,128)} %refs_2_.1, f32[32,72]{1,0:T(8,128)S(1)} %copy-done, f32[32,72]{1,0:T(8,128)S(1)} %copy-done.1), custom_call_target="tpu_custom_call" | custom-call | flops 10000000 | bytes 10000000 | tf_op jit(solution)/shard_map/hold/pallas_call | solution.py:237
  14.1 6.5 %all-to-all-done.refs_0_ = f32[8,8,128]{2,1,0:T(8,128)S(1)} async-done(((f32[8,8,128]{2,1,0:T(8,128)}), f32[8,8,128]{2,1,0:T(8,128)S(1)}, u32[]{:S(2)}, u32[]{:S(2)}) %all-to-all-start) | async-done | bytes 32800 | tf_op jit(solution)/shard_map/all_to_all | solution.py:38
  20.6 0.5 step.1
  21.1 16.7 %all_to_all.20.given_ref = f32[16,8,1152]{2,1,0:T(8,128)S(1)} all-to-all(f32[16,8,1152]{2,1,0:T(8,128)S(1)} %get-tuple-element.22), channel_id=1, replica_groups=mesh['zl'=2,'yh'=4,'yl'=2,'x'=4,'fz'=4,'fc'=2] {'zl','x','yl'}, dimensions={0} | all-to-all | bytes 1179648 | tf_op jit(solution)/shard_map/all_to_all | solution.py:38
  37.8 0.7 %copies.1._after = f32[4,8,1152]{2,1,0:T(8,128)} custom-call(f32[16,8,1152]{2,1,0:T(8,128)S(1)} %all_to_all.20.given_ref), custom_call_target="tpu_custom_call" | custom-call | tf_op jit(solution)/shard_map/copies/pallas_call | solution.py:158
  38.6 6.2 %all-to-all-start.2 = ((f32[4,8,1152]{2,1,0:T(8,128)}), f32[4,8,1152]{2,1,0:T(8,128)S(1)}, u32[]{:S(2)}, u32[]{:S(2)}) async-start(f32[4,8,1152]{2,1,0:T(8,128)} %copies.1._after), calls=%async_computation.2 | async-start | bytes 294912 | tf_op jit(solution)/shard_map/all_to_all | solution.py:38
  44.8 1.1 %write.1 = (f32[1,32,4608]{2,1,0:T(8,128)}, f32[1,32,4608]{2,1,0:T(8,128)}, f32[8,128]{1,0:T(8,128)S(1)}) custom-call(f32[1,32,4608]{2,1,0:T(8,128)S(1)} %get-tuple-element.23.first_ref, f32[1,32,4608]{2,1,0:T(8,128)S(1)} %get-tuple-element.24.second_ref, f32[4,8,1152]{2,1,0:T(8,128)} %copies.1._after), custom_call_target="tpu_custom_call" | custom-call | flops 1000000 | bytes 4000000 | tf_op jit(solution)/shard_map/write/pallas_call | solution.py:182
  45.8 7.8 %all-to-all-done.2.given_ref = f32[4,8,1152]{2,1,0:T(8,128)S(1)} async-done(((f32[4,8,1152]{2,1,0:T(8,128)}), f32[4,8,1152]{2,1,0:T(8,128)S(1)}, u32[]{:S(2)}, u32[]{:S(2)}) %all-to-all-start.2) | async-done | bytes 147488 | tf_op jit(solution)/shard_map/all_to_all | solution.py:38
  53.7 12.5 %all_to_all.21 = f32[16,8,1152]{2,1,0:T(8,128)S(1)} all-to-all(f32[16,8,1152]{2,1,0:T(8,128)S(1)} %sum.1), channel_id=1, replica_groups=mesh['zl'=2,'yh'=4,'yl'=2,'x'=4,'fz'=4,'fc'=2] {'zl','x','yl'}, dimensions={0} | all-to-all | bytes 1179648 | tf_op jit(solution)/shard_map/all_to_all | solution.py:38
  66.2 0.9 %outer.1 = (f32[32,4608]{1,0:T(8,128)}, f32[32,72]{1,0:T(8,128)}) custom-call(f32[32,4608]{1,0:T(8,128)S(1)} %bitcast.5, f32[32,72]{1,0:T(8,128)S(1)} %copy-done, f32[32,72]{1,0:T(8,128)S(1)} %copy-done.1), custom_call_target="tpu_custom_call" | custom-call | tf_op jit(solution)/shard_map/outer/pallas_call | solution.py:269
  (1 shorter events, 0.0 us)
Async XLA Ops:
  2.2 10.3 %copy-start = (f32[32,72]{1,0:T(8,128)S(1)}, f32[32,72]{1,0:T(8,128)}, u32[]{:S(2)}) copy-start(f32[32,72]{1,0:T(8,128)} %anchor_ref.1) | copy-start | bytes 27652
  2.2 10.3 %copy-start.1 = (f32[32,72]{1,0:T(8,128)S(1)}, f32[32,72]{1,0:T(8,128)}, u32[]{:S(2)}) copy-start(f32[32,72]{1,0:T(8,128)} %outer_ref.1) | copy-start | bytes 27652
  2.3 18.3 %all-to-all-start = ((f32[8,8,128]{2,1,0:T(8,128)}), f32[8,8,128]{2,1,0:T(8,128)S(1)}, u32[]{:S(2)}, u32[]{:S(2)}) async-start(f32[8,8,128]{2,1,0:T(8,128)} %get-tuple-element.17), calls=%async_computation | async-start | bytes 65536 | tf_op jit(solution)/shard_map/all_to_all | solution.py:38
  38.6 15.1 %all-to-all-start.2 = ((f32[4,8,1152]{2,1,0:T(8,128)}), f32[4,8,1152]{2,1,0:T(8,128)S(1)}, u32[]{:S(2)}, u32[]{:S(2)}) async-start(f32[4,8,1152]{2,1,0:T(8,128)} %copies.1._after), calls=%async_computation.2 | async-start | bytes 294912 | tf_op jit(solution)/shard_map/all_to_all | solution.py:38

commit v4 on v3

--- a/solution.py
+++ b/solution.py
@@ -42,26 +42,6 @@
     return pltpu.with_memory_space_constraint(value, pltpu.HBM)
 
 
-def square_kernel(grads_ref, parts_ref, held_ref, arrived):
-    rows, width = grads_ref.shape[1:]
-    step = 2 * SUB
-    cut = width // PIECES
-    pieces = [(top, at) for top in range(0, rows, step) for at in range(0, width, cut)]
-    copies = []
-    for i, (top, at) in enumerate(pieces):
-        here = (0, slice(top, top + step), slice(at, at + cut))
-        copies.append(pltpu.make_async_copy(grads_ref.at[here], held_ref.at[here], arrived.at[i]))
-        copies[-1].start()
-    total = jnp.zeros((step, LANE), f32)
-    for copy, (top, at) in zip(copies, pieces):
-        copy.wait()
-        for lane in range(at, at + cut, LANE):
-            tile = held_ref[0, top : top + step, lane : lane + LANE].astype(f32)
-            total += tile * tile
-    tile = total[:SUB] + total[SUB:]
-    parts_ref[...] = jnp.broadcast_to(tile[None], parts_ref.shape)
-
-
 def first_column(columns):
     index = 0
     for axis in REP:
@@ -75,27 +55,52 @@
     return start, first - start
 
 
-def hold_kernel(
-    scale, weights_ref, first_ref, second_ref, anchor_ref, outer_ref, base_ref, old_first_ref, old_second_ref, arrived
+def load_kernel(
+    scale, grads_ref, weights_ref, first_ref, second_ref, anchor_ref, outer_ref,
+    parts_ref, held_ref, base_ref, old_first_ref, old_second_ref, old_anchor_ref, old_outer_ref, arrived,
 ):
-    copies = []
-    pairs = ((weights_ref, base_ref), (first_ref, old_first_ref), (second_ref, old_second_ref))
-    for i, (given, held) in enumerate(pairs):
-        copies.append(pltpu.make_async_copy(given, held, arrived.at[i]))
-        copies[-1].start()
-    rows, width = base_ref.shape[1:]
-    mine = keep * anchor_ref[...] - drag * outer_ref[...]
+    rows, width = grads_ref.shape[1:]
+    step = 2 * SUB
+    cut = width // PIECES
+    pieces = [(0, slice(top, top + step), slice(at, at + cut)) for top in range(0, rows, step) for at in range(0, width, cut)]
+    count = 0
+
+    def fetch(given, held):
+        nonlocal count
+        copy = pltpu.make_async_copy(given, held, arrived.at[count])
+        copy.start()
+        count += 1
+        return copy
+
+    grads = [fetch(grads_ref.at[here], held_ref.at[here]) for here in pieces]
+    weights = [fetch(weights_ref.at[here], base_ref.at[here]) for here in pieces[::PIECES] for here in [here[:2]]]
+    small = [fetch(anchor_ref, old_anchor_ref), fetch(outer_ref, old_outer_ref)]
+    others = [
+        fetch(given.at[here[:2]], held.at[here[:2]])
+        for given, held in ((first_ref, old_first_ref), (second_ref, old_second_ref))
+        for here in pieces[::PIECES]
+    ]
+    total = jnp.zeros((step, LANE), f32)
+    for copy, (_, row, column) in zip(grads, pieces):
+        copy.wait()
+        for lane in range(column.start, column.stop, LANE):
+            tile = held_ref[0, row, lane : lane + LANE].astype(f32)
+            total += tile * tile
+    tile = total[:SUB] + total[SUB:]
+    parts_ref[...] = jnp.broadcast_to(tile[None], parts_ref.shape)
+    for copy in small:
+        copy.wait()
+    mine = keep * old_anchor_ref[...] - drag * old_outer_ref[...]
     columns = mine.shape[1]
     start, shift = window(first_column(columns), width)
     mine = jnp.concatenate([mine, jnp.zeros((rows, 2 * LANE - columns), f32)], axis=1)
     mine = pltpu.roll(mine, shift, 1)
-    copies[0].wait()
+    for copy in weights:
+        copy.wait()
     base_ref[...] = (scale * (1.0 - inner_rate * weight_decay)) * base_ref[...]
     base_ref[0, :, pl.ds(start, 2 * LANE)] += mine
-    copies[1].wait()
-    old_first_ref[...] = beta_one * old_first_ref[...]
-    copies[2].wait()
-    old_second_ref[...] = beta_two * old_second_ref[...]
+    for copy in others:
+        copy.wait()
 
 
 def step_kernel(
@@ -113,8 +118,8 @@
         for at in range(cuts):
             here = (0, slice(top, top + 2 * SUB), slice(at * cut, (at + 1) * cut))
             clipped = grads_ref[here].astype(f32) * clip_row
-            new_first = old_first_ref[here] + (1.0 - beta_one) * clipped
-            new_second = old_second_ref[here] + (1.0 - beta_two) * clipped * clipped
+            new_first = beta_one * old_first_ref[here] + (1.0 - beta_one) * clipped
+            new_second = beta_two * old_second_ref[here] + (1.0 - beta_two) * clipped * clipped
             new_first_ref[here] = new_first
             new_second_ref[here] = new_second
             block = base_ref[here] - (scale * inner_rate) * (new_first / (jnp.sqrt(new_second) + adam_eps))
@@ -191,11 +196,19 @@
     )(first, second, after)
 
 
-def outer_kernel(full_ref, anchor_ref, outer_ref, params_ref, momentum_ref, own_ref, done):
+def outer_kernel(
+    full_ref, anchor_ref, outer_ref, first_ref, second_ref, params_ref, momentum_ref, new_first_ref, new_second_ref,
+    own_ref, done,
+):
     copies = []
+    for given, out in ((first_ref, new_first_ref), (second_ref, new_second_ref)):
+        for at in range(0, given.shape[1], SUB):
+            here = (0, slice(at, at + SUB))
+            copies.append(pltpu.make_async_copy(given.at[here], out.at[here], done.at[len(copies)]))
+            copies[-1].start()
     for at in range(full_ref.shape[0] // SUB):
         here = slice(at * SUB, (at + 1) * SUB)
-        copies.append(pltpu.make_async_copy(full_ref.at[here], params_ref.at[here], done.at[at]))
+        copies.append(pltpu.make_async_copy(full_ref.at[here], params_ref.at[here], done.at[len(copies)]))
         copies[-1].start()
     columns = anchor_ref.shape[1]
     start, shift = window(first_column(columns), full_ref.shape[1])
@@ -220,30 +233,21 @@
     cuts = near // groups
     scale = gain / replicas
 
-    parts, grads = pl.pallas_call(
-        square_kernel,
-        out_shape=(pltpu.VMEM((shards, SUB, LANE), f32), pltpu.VMEM(grads.shape, grads.dtype)),
-        in_specs=[ANY],
-        out_specs=(VMEM, VMEM),
-        scratch_shapes=[pltpu.SemaphoreType.DMA((rows // (2 * SUB) * PIECES,))],
-        compiler_params=SMALL,
-        name="square",
-    )(in_hbm(grads))
+    def load(*refs):
+        load_kernel(scale, *refs)
+
+    given = (grads, inner_weights, first_moment, second_moment, anchor, outer_momentum)
+    pieces = rows // (2 * SUB)
+    parts, grads, base, old_first, old_second, anchor, outer_momentum = pl.pallas_call(
+        load,
+        out_shape=(pltpu.VMEM((shards, SUB, LANE), f32),) + tuple(pltpu.VMEM(a.shape, a.dtype) for a in given),
+        in_specs=[ANY] * 6,
+        out_specs=(VMEM,) * 7,
+        scratch_shapes=[pltpu.SemaphoreType.DMA((pieces * (PIECES + 3) + 2,))],
+        compiler_params=SMALL,
+        name="load",
+    )(*(in_hbm(a) for a in given))
     parts = exchange(parts, FSDP)
-
-    def hold(*refs):
-        hold_kernel(scale, *refs)
-
-    held = pl.pallas_call(
-        hold,
-        out_shape=(pltpu.VMEM((1, rows, width), f32),) * 3,
-        in_specs=[ANY, ANY, ANY, VMEM, VMEM],
-        out_specs=(VMEM,) * 3,
-        scratch_shapes=[pltpu.SemaphoreType.DMA((3,))],
-        compiler_params=SMALL,
-        cost_estimate=pl.CostEstimate(flops=10**7, bytes_accessed=10**7, transcendentals=0),
-        name="hold",
-    )(in_hbm(inner_weights), in_hbm(first_moment), in_hbm(second_moment), anchor, outer_momentum)
 
     def step(*refs):
         step_kernel(scale, rows * width * shards, *refs)
@@ -260,21 +264,21 @@
         input_output_aliases={3: 1, 4: 2},
         compiler_params=SMALL,
         name="step",
-    )(parts, grads, *held)
-    mine = sum_copies(exchange(blocks, NEAR), far)
-    new_first, new_second, mark = write_moments(new_first, new_second, mine)
-    mine = sum_spread(exchange(mine, FAR), near, mark)
+    )(parts, grads, base, old_first, old_second)
+    mine = sum_spread(exchange(blocks, NEAR), far)
+    mine = sum_spread(exchange(mine, FAR), near)
     full = exchange(mine, NEAR)
     full = full.reshape(groups, cuts, SUB, width // cuts).transpose(0, 2, 1, 3).reshape(rows, width)
-    new_params, new_momentum = pl.pallas_call(
+    new_params, new_momentum, new_first, new_second = pl.pallas_call(
         outer_kernel,
-        out_shape=(jax.ShapeDtypeStruct((rows, width), f32), jax.ShapeDtypeStruct((rows, columns), f32)),
-        in_specs=[VMEM] * 3,
-        out_specs=(ANY, ANY),
-        scratch_shapes=[pltpu.VMEM((rows, columns), f32), pltpu.SemaphoreType.DMA((groups + 1,))],
+        out_shape=(jax.ShapeDtypeStruct((rows, width), f32), jax.ShapeDtypeStruct((rows, columns), f32))
+        + (jax.ShapeDtypeStruct((1, rows, width), f32),) * 2,
+        in_specs=[VMEM] * 5,
+        out_specs=(ANY,) * 4,
+        scratch_shapes=[pltpu.VMEM((rows, columns), f32), pltpu.SemaphoreType.DMA((3 * groups + 1,))],
         compiler_params=SMALL,
         name="outer",
-    )(full, anchor, outer_momentum)
+    )(full, anchor, outer_momentum, new_first, new_second)
     return (new_params, new_momentum, new_first, new_second)
 
 

time: 67.5 us -> 67.3 us (level)
  blocking collectives: 29.2 us -> 62.6 us
  starting transfers between devices: 16.5 us -> 0 us
  waiting for transfers between devices: 14.3 us -> 0 us
  Pallas kernels: 6.31 us -> 3.69 us
    all_to_all x2 -> x4, blocking collectives: 29.2 us -> 62.6 us  [exchange(): return lax.all_to_all(value, axes, 0, 0, tiled=True)]
    all_to_all x2 -> x0, starting transfers between devices: 16.5 us -> none  [exchange(): return lax.all_to_all(value, axes, 0, 0, tiled=True)]
    all_to_all x2 -> x0, waiting for transfers between devices: 14.3 us -> none  [exchange(): return lax.all_to_all(value, axes, 0, 0, tiled=True)]
    pallas_call x4 -> x1, Pallas kernels: 4.91 us -> 1.74 us  [body(): pl.pallas_call(load, out_shape=(pltpu.VMEM((shards, SUB, LANE), f32),) +...]
  transfers between devices with their start and end apart: 2 -> 0, of which waited for: 2 -> 0; matrix products, arithmetic and copies ran while one was open for 0% -> 0% of each run, Pallas kernels for 4% -> 0%
where the time goes in v4:
time: 67.3 us; the launch traced here: 67 us
  blocking collectives  62.6 us (93%)
  Pallas kernels  3.69 us (5%)
    all_to_all x4, blocking collectives, exchange(): return lax.all_to_all(value, axes, 0, 0, tiled=True)  62.6 us
    pallas_call x1, Pallas kernels, body(): pl.pallas_call(load, out_shape=(pltpu.VMEM((shards, SUB, LANE), f32),) +...  1.74 us

profile of v4, /device:TPU:2, one launch (start us, length us, event | category | flops | bytes accessed | tf_op | source)
XLA Modules:
  0.0 67.0 jit_solution(10952238399479652134)
XLA Ops:
  0.6 1.7 %load.1 = (f32[8,8,128]{2,1,0:T(8,128)S(1)}, bf16[1,32,4608]{2,1,0:T(8,128)(2,1)S(1)}, f32[1,32,4608]{2,1,0:T(8,128)S(1)}, f32[1,32,4608]{2,1,0:T(8,128)S(1)}, f...) custom-call(bf16[1,32,4608]{2,1,0:T(8,128)(2,1)} %refs_0_.1, f32[1,32,4608]{2,1,0:T(8,128)} %refs_1_.1, ...), custom_call_target="tpu_custom_call" | custom-call | tf_op jit(solution)/shard_map/load/pallas_call | solution.py:241
  2.4 18.1 %all_to_all.20.refs_0_ = f32[8,8,128]{2,1,0:T(8,128)S(1)} all-to-all(f32[8,8,128]{2,1,0:T(8,128)S(1)} %get-tuple-element.14), channel_id=1, replica_groups=mesh['zl'=2,'yh'=4,'yl'=2,'x'=4,'fz'=4,'fc'=2] {'fz','fc'}, dimensions={0} | all-to-all | bytes 65536 | tf_op jit(solution)/shard_map/all_to_all | solution.py:38
  20.5 0.6 step.1
  21.1 16.7 %all_to_all.21.given_ref = f32[16,8,1152]{2,1,0:T(8,128)S(1)} all-to-all(f32[16,8,1152]{2,1,0:T(8,128)S(1)} %get-tuple-element.19), channel_id=1, replica_groups=mesh['zl'=2,'yh'=4,'yl'=2,'x'=4,'fz'=4,'fc'=2] {'zl','x','yl'}, dimensions={0} | all-to-all | bytes 1179648 | tf_op jit(solution)/shard_map/all_to_all | solution.py:38
  37.8 14.9 %all_to_all.22.given_ref = f32[4,8,1152]{2,1,0:T(8,128)S(1)} all-to-all(f32[4,8,1152]{2,1,0:T(8,128)S(1)} %sum.2), channel_id=1, replica_groups=mesh['zl'=2,'yh'=4,'yl'=2,'x'=4,'fz'=4,'fc'=2] {'yh'}, dimensions={0} | all-to-all | bytes 294912 | tf_op jit(solution)/shard_map/all_to_all | solution.py:38
  52.7 12.9 %all_to_all.23 = f32[16,8,1152]{2,1,0:T(8,128)S(1)} all-to-all(f32[16,8,1152]{2,1,0:T(8,128)S(1)} %sum.3), channel_id=1, replica_groups=mesh['zl'=2,'yh'=4,'yl'=2,'x'=4,'fz'=4,'fc'=2] {'zl','x','yl'}, dimensions={0} | all-to-all | bytes 1179648 | tf_op jit(solution)/shard_map/all_to_all | solution.py:38
  65.7 1.3 %outer.1 = (f32[32,4608]{1,0:T(8,128)}, f32[32,72]{1,0:T(8,128)}, f32[1,32,4608]{2,1,0:T(8,128)}, f32[1,32,4608]{2,1,0:T(8,128)}) custom-call(f32[32,4608]{1,0:T(8,128)S(1)} %bitcast.5, f32[32,72]{1,0:T(8,128)S(1)} %get-tuple-element.20.anchor_ref, f32[32,72]{1,0:T(8,128)S(1)} %get-tuple-element.21.outer_ref, ...), custom_call_target="tpu_custom_call" | custom-call | tf_op jit(solution)/shard_map/outer/pallas_call | solution.py:272
  (2 shorter events, 0.1 us)

commit v5 on v4

--- a/solution.py
+++ b/solution.py
@@ -27,7 +27,8 @@
 drag = outer_rate * outer_beta * outer_beta
 
 SUB, LANE = 8, 128
-PIECES = 4
+PIECES = 2
+SHARES = 1
 SMALL = pltpu.CompilerParams(vmem_limit_bytes=4 * 2**20)
 VMEM = pl.BlockSpec(memory_space=pltpu.VMEM)
 ANY = pl.BlockSpec(memory_space=pl.ANY)
@@ -55,58 +56,48 @@
     return start, first - start
 
 
-def load_kernel(
-    scale, grads_ref, weights_ref, first_ref, second_ref, anchor_ref, outer_ref,
-    parts_ref, held_ref, base_ref, old_first_ref, old_second_ref, old_anchor_ref, old_outer_ref, arrived,
-):
+def load_kernel(grads_ref, *refs):
+    *given, parts_ref, grads_held = refs[: len(refs) // 2 + 1]
+    *held, arrived = refs[len(refs) // 2 + 1 :]
     rows, width = grads_ref.shape[1:]
     step = 2 * SUB
     cut = width // PIECES
-    pieces = [(0, slice(top, top + step), slice(at, at + cut)) for top in range(0, rows, step) for at in range(0, width, cut)]
     count = 0
 
-    def fetch(given, held):
+    def fetch(source, target):
         nonlocal count
-        copy = pltpu.make_async_copy(given, held, arrived.at[count])
+        copy = pltpu.make_async_copy(source, target, arrived.at[count])
         copy.start()
         count += 1
         return copy
 
-    grads = [fetch(grads_ref.at[here], held_ref.at[here]) for here in pieces]
-    weights = [fetch(weights_ref.at[here], base_ref.at[here]) for here in pieces[::PIECES] for here in [here[:2]]]
-    small = [fetch(anchor_ref, old_anchor_ref), fetch(outer_ref, old_outer_ref)]
-    others = [
-        fetch(given.at[here[:2]], held.at[here[:2]])
-        for given, held in ((first_ref, old_first_ref), (second_ref, old_second_ref))
-        for here in pieces[::PIECES]
-    ]
+    pieces = [(0, slice(top, top + step), slice(at, at + cut)) for top in range(0, rows, step) for at in range(0, width, cut)]
+    grads = [fetch(grads_ref.at[here], grads_held.at[here]) for here in pieces]
+    others = []
+    for source, target in zip(given, held):
+        if len(source.shape) == 3:
+            size = rows // SHARES
+            for top in range(0, rows, size):
+                others.append(fetch(source.at[0, top : top + size], target.at[0, top : top + size]))
+        else:
+            others.append(fetch(source, target))
     total = jnp.zeros((step, LANE), f32)
     for copy, (_, row, column) in zip(grads, pieces):
         copy.wait()
         for lane in range(column.start, column.stop, LANE):
-            tile = held_ref[0, row, lane : lane + LANE].astype(f32)
+            tile = grads_held[0, row, lane : lane + LANE].astype(f32)
             total += tile * tile
     tile = total[:SUB] + total[SUB:]
-    parts_ref[...] = jnp.broadcast_to(tile[None], parts_ref.shape)
-    for copy in small:
-        copy.wait()
-    mine = keep * old_anchor_ref[...] - drag * old_outer_ref[...]
-    columns = mine.shape[1]
-    start, shift = window(first_column(columns), width)
-    mine = jnp.concatenate([mine, jnp.zeros((rows, 2 * LANE - columns), f32)], axis=1)
-    mine = pltpu.roll(mine, shift, 1)
-    for copy in weights:
-        copy.wait()
-    base_ref[...] = (scale * (1.0 - inner_rate * weight_decay)) * base_ref[...]
-    base_ref[0, :, pl.ds(start, 2 * LANE)] += mine
+    parts_ref[...] = jnp.broadcast_to(jnp.sum(tile, axis=0, keepdims=True), parts_ref.shape)
     for copy in others:
         copy.wait()
 
 
 def step_kernel(
-    scale, entries, parts_ref, grads_ref, base_ref, old_first_ref, old_second_ref, blocks_ref, new_first_ref, new_second_ref
+    scale, entries, parts_ref, grads_ref, weights_ref, first_ref, second_ref, anchor_ref, outer_ref,
+    blocks_ref, new_first_ref, new_second_ref,
 ):
-    rows, width = base_ref.shape[1:]
+    rows, width = weights_ref.shape[1:]
     cut = blocks_ref.shape[2]
     cuts = width // cut
     norm_square = jnp.sum(parts_ref[...])
@@ -118,13 +109,23 @@
         for at in range(cuts):
             here = (0, slice(top, top + 2 * SUB), slice(at * cut, (at + 1) * cut))
             clipped = grads_ref[here].astype(f32) * clip_row
-            new_first = beta_one * old_first_ref[here] + (1.0 - beta_one) * clipped
-            new_second = beta_two * old_second_ref[here] + (1.0 - beta_two) * clipped * clipped
+            new_first = beta_one * first_ref[here] + (1.0 - beta_one) * clipped
+            new_second = beta_two * second_ref[here] + (1.0 - beta_two) * clipped * clipped
             new_first_ref[here] = new_first
             new_second_ref[here] = new_second
-            block = base_ref[here] - (scale * inner_rate) * (new_first / (jnp.sqrt(new_second) + adam_eps))
+            block = (scale * (1.0 - inner_rate * weight_decay)) * weights_ref[here]
+            block -= (scale * inner_rate) * (new_first / (jnp.sqrt(new_second) + adam_eps))
             for half in range(2):
                 blocks_ref[(top // SUB + half) * cuts + at] = block[half * SUB : (half + 1) * SUB]
+    mine = keep * anchor_ref[...] - drag * outer_ref[...]
+    columns = mine.shape[1]
+    first = first_column(columns)
+    block = first // cut
+    start, shift = window(first - block * cut, cut)
+    mine = jnp.concatenate([mine, jnp.zeros((rows, 2 * LANE - columns), f32)], axis=1)
+    mine = pltpu.roll(mine, shift, 1)
+    for group in range(rows // SUB):
+        blocks_ref[group * cuts + block, :, pl.ds(start, 2 * LANE)] += mine[group * SUB : (group + 1) * SUB]
 
 
 def sum_kernel(given_ref, *refs):
@@ -174,8 +175,8 @@
 def write_kernel(first_ref, second_ref, _after, new_first_ref, new_second_ref, mark_ref, done):
     copies = []
     for given, out in ((first_ref, new_first_ref), (second_ref, new_second_ref)):
-        for at in range(0, given.shape[1], SUB):
-            here = (0, slice(at, at + SUB))
+        for at in range(0, given.shape[1], 2 * SUB):
+            here = (0, slice(at, at + 2 * SUB))
             copies.append(pltpu.make_async_copy(given.at[here], out.at[here], done.at[len(copies)]))
             copies[-1].start()
     mark_ref[...] = jnp.zeros(mark_ref.shape, f32)
@@ -202,8 +203,8 @@
 ):
     copies = []
     for given, out in ((first_ref, new_first_ref), (second_ref, new_second_ref)):
-        for at in range(0, given.shape[1], SUB):
-            here = (0, slice(at, at + SUB))
+        for at in range(0, given.shape[1], 2 * SUB):
+            here = (0, slice(at, at + 2 * SUB))
             copies.append(pltpu.make_async_copy(given.at[here], out.at[here], done.at[len(copies)]))
             copies[-1].start()
     for at in range(full_ref.shape[0] // SUB):
@@ -233,20 +234,18 @@
     cuts = near // groups
     scale = gain / replicas
 
-    def load(*refs):
-        load_kernel(scale, *refs)
-
     given = (grads, inner_weights, first_moment, second_moment, anchor, outer_momentum)
     pieces = rows // (2 * SUB)
-    parts, grads, base, old_first, old_second, anchor, outer_momentum = pl.pallas_call(
-        load,
-        out_shape=(pltpu.VMEM((shards, SUB, LANE), f32),) + tuple(pltpu.VMEM(a.shape, a.dtype) for a in given),
+    parts, *given = pl.pallas_call(
+        load_kernel,
+        out_shape=(pltpu.VMEM((shards, LANE), f32),) + tuple(pltpu.VMEM(a.shape, a.dtype) for a in given),
         in_specs=[ANY] * 6,
         out_specs=(VMEM,) * 7,
-        scratch_shapes=[pltpu.SemaphoreType.DMA((pieces * (PIECES + 3) + 2,))],
+        scratch_shapes=[pltpu.SemaphoreType.DMA((pieces * PIECES + 3 * SHARES + 2,))],
         compiler_params=SMALL,
         name="load",
     )(*(in_hbm(a) for a in given))
+    grads, inner_weights, first_moment, second_moment, anchor, outer_momentum = given
     parts = exchange(parts, FSDP)
 
     def step(*refs):
@@ -259,12 +258,12 @@
             pltpu.VMEM((1, rows, width), f32),
             pltpu.VMEM((1, rows, width), f32),
         ),
-        in_specs=[VMEM] * 5,
+        in_specs=[VMEM] * 7,
         out_specs=(VMEM,) * 3,
         input_output_aliases={3: 1, 4: 2},
         compiler_params=SMALL,
         name="step",
-    )(parts, grads, base, old_first, old_second)
+    )(parts, grads, inner_weights, first_moment, second_moment, anchor, outer_momentum)
     mine = sum_spread(exchange(blocks, NEAR), far)
     mine = sum_spread(exchange(mine, FAR), near)
     full = exchange(mine, NEAR)

time: 67.3 us -> 67 us (level)
  no operation moved by 1% of the time
where the time goes in v5:
time: 67 us; the launch traced here: 66.7 us
  blocking collectives  62.4 us (93%)
  Pallas kernels  3.65 us (5%)
    all_to_all x4, blocking collectives, exchange(): return lax.all_to_all(value, axes, 0, 0, tiled=True)  62.4 us
    pallas_call x1, Pallas kernels, body(): pl.pallas_call(load_kernel, out_shape=(pltpu.VMEM((shards, LANE), f32),)...  1.66 us

profile of v5, /device:TPU:2, one launch (start us, length us, event | category | flops | bytes accessed | tf_op | source)
XLA Modules:
  0.0 66.7 jit_solution(487607135638881865)
XLA Ops:
  0.6 1.7 %load.1 = (f32[8,128]{1,0:T(8,128)S(1)}, bf16[1,32,4608]{2,1,0:T(8,128)(2,1)S(1)}, f32[1,32,4608]{2,1,0:T(8,128)S(1)}, f32[1,32,4608]{2,1,0:T(8,128)S(1)}, f32[1...) custom-call(bf16[1,32,4608]{2,1,0:T(8,128)(2,1)} %grads_ref.1, f32[1,32,4608]{2,1,0:T(8,128)} %refs_0_.1, ...), custom_call_target="tpu_custom_call" | custom-call | tf_op jit(solution)/shard_map/load/pallas_call | solution.py:239
  2.3 17.8 %all_to_all.26 = f32[8,1,128]{2,1,0:T(1,128)S(1)} all-to-all(f32[8,1,128]{2,1,0:T(1,128)S(1)} %bitcast.11), channel_id=1, replica_groups=mesh['zl'=2,'yh'=4,'yl'=2,'x'=4,'fz'=4,'fc'=2] {'fz','fc'}, dimensions={0} | all-to-all | bytes 8192 | tf_op jit(solution)/shard_map/all_to_all | solution.py:39
  20.1 0.6 step.1
  20.7 16.8 %all_to_all.27.given_ref = f32[16,8,1152]{2,1,0:T(8,128)S(1)} all-to-all(f32[16,8,1152]{2,1,0:T(8,128)S(1)} %get-tuple-element.21), channel_id=1, replica_groups=mesh['zl'=2,'yh'=4,'yl'=2,'x'=4,'fz'=4,'fc'=2] {'zl','x','yl'}, dimensions={0} | all-to-all | bytes 1179648 | tf_op jit(solution)/shard_map/all_to_all | solution.py:39
  37.6 14.9 %all_to_all.28.given_ref = f32[4,8,1152]{2,1,0:T(8,128)S(1)} all-to-all(f32[4,8,1152]{2,1,0:T(8,128)S(1)} %sum.2), channel_id=1, replica_groups=mesh['zl'=2,'yh'=4,'yl'=2,'x'=4,'fz'=4,'fc'=2] {'yh'}, dimensions={0} | all-to-all | bytes 294912 | tf_op jit(solution)/shard_map/all_to_all | solution.py:39
  52.5 12.9 %all_to_all.29 = f32[16,8,1152]{2,1,0:T(8,128)S(1)} all-to-all(f32[16,8,1152]{2,1,0:T(8,128)S(1)} %sum.3), channel_id=1, replica_groups=mesh['zl'=2,'yh'=4,'yl'=2,'x'=4,'fz'=4,'fc'=2] {'zl','x','yl'}, dimensions={0} | all-to-all | bytes 1179648 | tf_op jit(solution)/shard_map/all_to_all | solution.py:39
  65.4 1.3 %outer.1 = (f32[32,4608]{1,0:T(8,128)}, f32[32,72]{1,0:T(8,128)}, f32[1,32,4608]{2,1,0:T(8,128)}, f32[1,32,4608]{2,1,0:T(8,128)}) custom-call(f32[32,4608]{1,0:T(8,128)S(1)} %bitcast.9, f32[32,72]{1,0:T(8,128)S(1)} %get-tuple-element.19.refs_5_.anchor_ref, f32[32,72]{1,0:T(8,128)S(1)} %get-tuple-element.20.refs_6_.outer_ref, ...), custom_call_target="tpu_custom_call" | custom-call | tf_op jit(solution)/shard_map/outer/pallas_call | solution.py:271
  (2 shorter events, 0.1 us)

commit v6 on v5

--- a/solution.py
+++ b/solution.py
@@ -114,7 +114,7 @@
             new_first_ref[here] = new_first
             new_second_ref[here] = new_second
             block = (scale * (1.0 - inner_rate * weight_decay)) * weights_ref[here]
-            block -= (scale * inner_rate) * (new_first / (jnp.sqrt(new_second) + adam_eps))
+            block -= (scale * inner_rate) * (new_first / (new_second * lax.rsqrt(new_second) + adam_eps))
             for half in range(2):
                 blocks_ref[(top // SUB + half) * cuts + at] = block[half * SUB : (half + 1) * SUB]
     mine = keep * anchor_ref[...] - drag * outer_ref[...]
@@ -234,18 +234,18 @@
     cuts = near // groups
     scale = gain / replicas
 
-    given = (grads, inner_weights, first_moment, second_moment, anchor, outer_momentum)
+    given = (grads, inner_weights, first_moment, second_moment)
     pieces = rows // (2 * SUB)
     parts, *given = pl.pallas_call(
         load_kernel,
         out_shape=(pltpu.VMEM((shards, LANE), f32),) + tuple(pltpu.VMEM(a.shape, a.dtype) for a in given),
-        in_specs=[ANY] * 6,
-        out_specs=(VMEM,) * 7,
-        scratch_shapes=[pltpu.SemaphoreType.DMA((pieces * PIECES + 3 * SHARES + 2,))],
+        in_specs=[ANY] * 4,
+        out_specs=(VMEM,) * 5,
+        scratch_shapes=[pltpu.SemaphoreType.DMA((pieces * PIECES + 3 * SHARES,))],
         compiler_params=SMALL,
         name="load",
     )(*(in_hbm(a) for a in given))
-    grads, inner_weights, first_moment, second_moment, anchor, outer_momentum = given
+    grads, inner_weights, first_moment, second_moment = given
     parts = exchange(parts, FSDP)
 
     def step(*refs):

time: 67 us -> 66.9 us (level)
  no operation moved by 1% of the time
where the time goes in v6:
time: 66.9 us; the launch traced here: 66.6 us
  blocking collectives  62.4 us (93%)
  Pallas kernels  3.54 us (5%)
  between operations  0.67 us (1%)
    all_to_all x4, blocking collectives, exchange(): return lax.all_to_all(value, axes, 0, 0, tiled=True)  62.4 us
    pallas_call x1, Pallas kernels, body(): pl.pallas_call(load_kernel, out_shape=(pltpu.VMEM((shards, LANE), f32),)...  1.64 us

profile of v6, /device:TPU:2, one launch (start us, length us, event | category | flops | bytes accessed | tf_op | source)
XLA Modules:
  0.0 66.6 jit_solution(15176622470479635886)
XLA Ops:
  0.6 0.0 copy-start.1
  0.6 1.6 %load.1 = (f32[8,128]{1,0:T(8,128)S(1)}, bf16[1,32,4608]{2,1,0:T(8,128)(2,1)S(1)}, f32[1,32,4608]{2,1,0:T(8,128)S(1)}, f32[1,32,4608]{2,1,0:T(8,128)S(1)}, f32[1,32,4608]{2,1,0:T(8,128)S(1)}) custom-call(bf16[1,32,4608]{2,1,0:T(8,128)(2,1)} %grads_ref.1, f32[1,32,4608]{2,1,0:T(8,128)} %refs_0_.1, f32[1,32,4608]{2,1,0:T(8,128)} %refs_1_.1, f32[1,32,4608]{2,1,0:T(8,128)} %refs_2_.1), custom_call_target="tpu_custom_call" | custom-call | tf_op jit(solution)/shard_map/load/pallas_call | solution.py:239
  2.3 0.0 copy-start
  2.3 17.8 %all_to_all.26 = f32[8,1,128]{2,1,0:T(1,128)S(1)} all-to-all(f32[8,1,128]{2,1,0:T(1,128)S(1)} %bitcast.11), channel_id=1, replica_groups=mesh['zl'=2,'yh'=4,'yl'=2,'x'=4,'fz'=4,'fc'=2] {'fz','fc'}, dimensions={0} | all-to-all | bytes 8192 | tf_op jit(solution)/shard_map/all_to_all | solution.py:39
  20.1 0.0 copy-done.1
  20.1 0.0 copy-done
  20.1 0.5 step.1
  20.6 16.8 %all_to_all.27.given_ref = f32[16,8,1152]{2,1,0:T(8,128)S(1)} all-to-all(f32[16,8,1152]{2,1,0:T(8,128)S(1)} %get-tuple-element.17), channel_id=1, replica_groups=mesh['zl'=2,'yh'=4,'yl'=2,'x'=4,'fz'=4,'fc'=2] {'zl','x','yl'}, dimensions={0} | all-to-all | bytes 1179648 | tf_op jit(solution)/shard_map/all_to_all | solution.py:39
  37.5 14.9 %all_to_all.28.given_ref = f32[4,8,1152]{2,1,0:T(8,128)S(1)} all-to-all(f32[4,8,1152]{2,1,0:T(8,128)S(1)} %sum.2), channel_id=1, replica_groups=mesh['zl'=2,'yh'=4,'yl'=2,'x'=4,'fz'=4,'fc'=2] {'yh'}, dimensions={0} | all-to-all | bytes 294912 | tf_op jit(solution)/shard_map/all_to_all | solution.py:39
  52.4 12.9 %all_to_all.29 = f32[16,8,1152]{2,1,0:T(8,128)S(1)} all-to-all(f32[16,8,1152]{2,1,0:T(8,128)S(1)} %sum.3), channel_id=1, replica_groups=mesh['zl'=2,'yh'=4,'yl'=2,'x'=4,'fz'=4,'fc'=2] {'zl','x','yl'}, dimensions={0} | all-to-all | bytes 1179648 | tf_op jit(solution)/shard_map/all_to_all | solution.py:39
  65.3 1.3 %outer.1 = (f32[32,4608]{1,0:T(8,128)}, f32[32,72]{1,0:T(8,128)}, f32[1,32,4608]{2,1,0:T(8,128)}, f32[1,32,4608]{2,1,0:T(8,128)}) custom-call(f32[32,4608]{1,0:T(8,128)S(1)} %bitcast.9, f32[32,72]{1,0:T(8,128)S(1)} %copy-done, f32[32,72]{1,0:T(8,128)S(1)} %copy-done.1, f32[1,32,4608]{2,1,0:T(8,128)S(1)} %get-tuple-element.18.first_ref, ...), custom_call_target="tpu_custom_call" | custom-call | tf_op jit(solution)/shard_map/outer/pallas_call | solution.py:271
  (2 shorter events, 0.1 us)
Async XLA Ops:
  0.6 19.5 %copy-start.1 = (f32[32,72]{1,0:T(8,128)S(1)}, f32[32,72]{1,0:T(8,128)}, u32[]{:S(2)}) copy-start(f32[32,72]{1,0:T(8,128)} %outer_ref.1) | copy-start | bytes 27652
  2.3 17.8 %copy-start = (f32[32,72]{1,0:T(8,128)S(1)}, f32[32,72]{1,0:T(8,128)}, u32[]{:S(2)}) copy-start(f32[32,72]{1,0:T(8,128)} %anchor_ref.1) | copy-start | bytes 27652
